TPU v7x, 32 devices: a whole 2x2x4 slice. The times are simulated.
32 devices in a mesh: groups: 2 (over x), tile: 16 (over z, y, core).
Axes of the slice: x: 2, y: 2, z: 4, core: 2. Of those that a mesh axis runs over, the one named last changes fastest.
Arguments:
- log_conductivity: float32 [4, 128, 1024], P('groups', 'tile'), parts along dimension 0, may hold values from -2.9 to 3, as said below
- storage: float32 [4, 128, 1024], P('groups', 'tile'), parts along dimension 0, may hold values from 0.05 to 60
- recharge: float32 [4, 128, 1024], P('groups', 'tile'), parts along dimension 0, may hold values from -6 to 6
- observed: float32 [24, 400], P('groups'), parts along dimension 0, may hold values from -6 to 6
- rates: float32 [24], P('groups'), parts along dimension 0, may hold values from 2 to 8
- well_tile: int32 [400], replicated, may hold values from 0 to 15
- well_row: int32 [400], replicated, may hold values from 0 to 7
- well_col: int32 [400], replicated, may hold values from 0 to 1023
- well_screen: int32 [400, 2], replicated, may hold values from 0 to 2, as said below
- test_well: int32 [12], replicated, may hold values from 0 to 399
Outputs:
- gradient: float32 [4, 128, 1024], P('groups', 'tile'), parts along dimension 0
- predicted: float32 [24, 400], P('groups'), parts along dimension 0
There are 2 independent parts, one for each index of `groups`. A program takes and returns all parts, laid end to end along the dimension named above; an argument that names none is the same for every part. Nothing has to cross between parts.
Inputs may be any that keep to these rules, and one draw needn't show every extreme that they name: `log_conductivity`: log-conductivities rough from cell to cell. Each well's screen holds one or more whole layers, well_screen[w,0] < well_screen[w,1].
All inputs are finite; a program needn't handle non-finite values.
Results may differ from a plain program's by a relative error of at most 0.00014.
Values sent between devices are 32-bit elements; how exact they have to be, the bound alone decides.
A program may use at most 64 MiB of HBM per device.

v0:
```python
import jax
import jax.numpy as jnp
from jax import lax
from jax.sharding import PartitionSpec as P

ITERS = 4


def extended_2(block, sides, width):
    for axis, dim in sides:
        count = lax.axis_size(axis)
        forward = [(i, i + 1) for i in range(count - 1)]
        backward = [(target, source) for source, target in forward]
        low = lax.ppermute(
            lax.slice_in_dim(block, block.shape[dim] - width, None, axis=dim), axis, forward
        )
        high = lax.ppermute(lax.slice_in_dim(block, 0, width, axis=dim), axis, backward)
        block = jnp.concatenate([low, block, high], axis=dim)
    return block


def pad_axis(array, axis, before, after):
    widths = [(0, 0)] * array.ndim
    widths[axis] = (before, after)
    return jnp.pad(array, widths)


def faces_along(extended):
    return 0.5 * (extended[:, 1:, :] + extended[:, :-1, :])


def faces_other(conductivity):
    padded_y = pad_axis(conductivity, 2, 1, 1)
    faces_y = 0.5 * (padded_y[:, :, 1:] + padded_y[:, :, :-1])
    faces_z = 0.5 * (conductivity[1:] + conductivity[:-1])
    return (faces_y, faces_z)


def operate(padded, faces_x, faces_y, faces_z, store):
    field = padded[..., 1:-1, :]
    flux_x = faces_x * (padded[..., 1:, :] - padded[..., :-1, :])
    result = store * field + flux_x[..., :-1, :] - flux_x[..., 1:, :]
    padded_y = pad_axis(field, field.ndim - 1, 1, 1)
    flux_y = faces_y * (padded_y[..., 1:] - padded_y[..., :-1])
    result = result + flux_y[..., :-1] - flux_y[..., 1:]
    flux_z = faces_z * (field[..., 1:, :, :] - field[..., :-1, :, :])
    layer_axis = field.ndim - 3
    return result + pad_axis(flux_z, layer_axis, 1, 0) - pad_axis(flux_z, layer_axis, 0, 1)


def chebyshev(source, apply_op, low, high, valid):
    center = 0.5 * (high + low)
    radius = 0.5 * (high - low)
    spread = center / radius
    ratio = 1.0 / spread
    direction = source / center
    iterate = direction
    residual = source
    for turn in range(ITERS):
        residual = residual - apply_op(direction)
        ratio_next = 1.0 / (2.0 * spread - ratio)
        direction = (ratio_next * ratio * direction + 2.0 * ratio_next / radius * residual) * valid
        iterate = iterate + direction
        ratio = ratio_next
    return iterate


def local(
    log_conductivity,
    storage,
    recharge,
    observed,
    rates,
    well_tile,
    well_row,
    well_col,
    well_screen,
    test_well,
):
    layers_count, strip, columns = log_conductivity.shape
    tests = observed.shape[0]
    tile_index = lax.axis_index("tile")
    conductivity = jnp.exp(log_conductivity)
    depth = 1
    coefficients = extended_2(jnp.stack((conductivity, storage)), (("tile", 2),), depth)
    cond_ext = coefficients[0]
    own_x = faces_along(cond_ext)
    own_y, own_z = faces_other(conductivity)
    face_sum = own_x[:, :-1] + own_x[:, 1:] + own_y[:, :, :-1] + own_y[:, :, 1:]
    face_sum = face_sum + pad_axis(own_z, 0, 1, 0) + pad_axis(own_z, 0, 0, 1)
    local_high = jnp.max(storage + 2.0 * face_sum)
    local_low = jnp.min(storage)
    high = lax.pmax(local_high, "tile")
    low = lax.pmin(local_low, "tile")

    def solve(source):
        faces_x = faces_along(cond_ext)
        faces_y, faces_z = faces_other(conductivity)

        def apply_each(field):
            padded = extended_2(field, (("tile", 2),), 1)
            return operate(padded, faces_x, faces_y, faces_z, storage)

        return chebyshev(source, apply_each, low, high, jnp.float32(1.0))

    layers = jnp.arange(layers_count, dtype=jnp.int32)
    top = well_screen[:, 0]
    bottom = well_screen[:, 1]
    inside = ((layers[None, :] >= top[:, None]) & (layers[None, :] < bottom[:, None])).astype(
        jnp.float32
    )
    screen_weight = inside / (bottom - top).astype(jnp.float32)[:, None]
    owned = (well_tile == tile_index).astype(jnp.float32)
    owned_weight = screen_weight * owned[:, None]
    amounts = -rates[:, None] * owned_weight[test_well]
    test_rows = jnp.arange(tests, dtype=jnp.int32)[:, None]
    layer_rows = layers[None, :]
    pumping = jnp.zeros((tests, layers_count, strip, columns), jnp.float32)
    pumping = pumping.at[
        test_rows, layer_rows, well_row[test_well][:, None], well_col[test_well][:, None]
    ].add(amounts)
    heads = solve(recharge[None] + pumping)
    sampled = heads[:, :, well_row, well_col]
    local_heads = jnp.sum(sampled * owned_weight.T[None], axis=1)
    predicted = lax.psum(local_heads, "tile")
    misfit = predicted - observed
    scale = jnp.sqrt(jnp.mean(misfit * misfit) + 1e-06)
    weight = misfit / scale
    adjoint_source = jnp.zeros((tests, layers_count, strip, columns), jnp.float32)
    adjoint_source = adjoint_source.at[:, :, well_row, well_col].add(
        weight[:, None, :] * owned_weight.T[None]
    )
    adjoint = solve(adjoint_source)
    padded = extended_2(jnp.stack((heads, adjoint)), (("tile", 3),), 1)
    term_x = jnp.sum(
        0.5
        * (padded[1][:, :, 1:] - padded[1][:, :, :-1])
        * (padded[0][:, :, 1:] - padded[0][:, :, :-1]),
        axis=0,
    )
    x_sum = term_x[:, :-1] + term_x[:, 1:]
    padded_a = pad_axis(adjoint, 3, 1, 1)
    padded_h = pad_axis(heads, 3, 1, 1)
    term_y = jnp.sum(
        0.5 * (padded_a[..., 1:] - padded_a[..., :-1]) * (padded_h[..., 1:] - padded_h[..., :-1]),
        axis=0,
    )
    term_z = jnp.sum(
        0.5 * (adjoint[:, 1:] - adjoint[:, :-1]) * (heads[:, 1:] - heads[:, :-1]), axis=0
    )
    cell_sum = x_sum + term_y[:, :, :-1] + term_y[:, :, 1:]
    cell_sum = cell_sum + pad_axis(term_z, 0, 1, 0) + pad_axis(term_z, 0, 0, 1)
    gradient = -conductivity * cell_sum
    return (gradient, predicted)


def solution(mesh):
    return jax.shard_map(
        local,
        mesh=mesh,
        in_specs=(
            P("groups", "tile", None),
            P("groups", "tile", None),
            P("groups", "tile", None),
            P("groups", None),
            P("groups"),
            P(),
            P(),
            P(),
            P(),
            P(),
        ),
        out_specs=(P("groups", "tile", None), P("groups", None)),
        check_vma=False,
    )
```

profile of v0, /device:TPU:5, one launch (start us, length us, event | category | flops | bytes accessed | tf_op | source)
XLA Modules:
  0.0 294.1 jit_solution(15009678495756000687)
XLA Ops:
  0.6 0.9 exponential_bitcast_fusion
  1.5 0.9 pad_maximum_fusion.7
  2.5 3.7 %collective-permute-start = (f32[2,2,1,1024]{3,2,1,0:T(1,128)S(1)}, f32[2,2,1,1024]{3,2,1,0:T(1,128)S(1)}, u32[]{:S(2)}, u32[]{:S(2)}) collective-permute-start(f32[2,2,1,1024]{3,2,1,0:T(1,128)S(1)} %get-tuple-element.40), channel_id=1, source_target_pairs={{0,1},{1,2},{2,3},{3,4},{4,5},{5,6},{6,7},{7,8},{8,9},{9,10},{10,1... | collective-permute-start | bytes 49160 | tf_op jit(solution)/shard_map/ppermute | solution.py:14
  6.2 1.9 collective-permute-start.1
  8.1 0.7 compare_select_fusion.4
  8.8 0.7 compare_select_fusion.1
  9.5 0.7 compare_select_fusion
  10.2 1.3 gather_fusion.1
  11.5 1.3 gather_fusion
  12.9 0.8 fusion.93
  13.7 0.7 compare_convert_fusion
  14.7 0.6 gather_fusion.2
  15.8 2.9 scatter_fusion
  18.8 0.7 fusion.78
  19.5 25.8 %pmax.7 = f32[]{:T(128)} all-reduce(f32[]{:T(128)} %get-tuple-element.5), channel_id=1, replica_groups=mesh['groups'=2,'tile'=16] {'tile'}, use_global_device_ids=true, to_apply=%region_2.3 | all-reduce | flops 1 | bytes 8 | tf_op jit(solution)/shard_map/pmax | solution.py:93
  45.4 32.8 %pmin.7 = f32[]{:T(128)} all-reduce(f32[]{:T(128)} %get-tuple-element.4), channel_id=1, replica_groups=mesh['groups'=2,'tile'=16] {'tile'}, use_global_device_ids=true, to_apply=%region_4.5 | all-reduce | flops 1 | bytes 8 | tf_op jit(solution)/shard_map/pmin | solution.py:94
  79.5 0.8 fusion.92
  80.6 1.9 collective-permute-start.3
  82.5 2.6 collective-permute-start.2
  86.9 2.7 collective-permute-done.2
  89.6 1.2 fusion.3
  90.8 0.5 multiply_add_fusion.5
  91.8 1.9 collective-permute-start.5
  93.7 4.0 %collective-permute-start.4 = (f32[12,2,1,1024]{3,2,1,0:T(1,128)S(1)}, f32[12,2,1,1024]{3,2,1,0:T(1,128)S(1)}, u32[]{:S(2)}, u32[]{:S(2)}) collective-permute-start(f32[12,2,1,1024]{3,2,1,0:T(1,128)S(1)} %get-tuple-element.37), channel_id=1, source_target_pairs={{1,0},{2,1},{3,2},{4,3},{5,4},{6,5},{7,6},{8,7},{9,8},{10,9},{11,1... | collective-permute-start | bytes 294920 | tf_op jit(solution)/shard_map/ppermute | solution.py:17
  97.8 2.7 collective-permute-done.4
  100.8 0.5 multiply_add_fusion.4
  101.8 1.9 collective-permute-start.7
  103.7 3.3 %collective-permute-start.6 = (f32[12,2,1,1024]{3,2,1,0:T(1,128)S(1)}, f32[12,2,1,1024]{3,2,1,0:T(1,128)S(1)}, u32[]{:S(2)}, u32[]{:S(2)}) collective-permute-start(f32[12,2,1,1024]{3,2,1,0:T(1,128)S(1)} %get-tuple-element.35), channel_id=1, source_target_pairs={{1,0},{2,1},{3,2},{4,3},{5,4},{6,5},{7,6},{8,7},{9,8},{10,9},{11,1... | collective-permute-start | bytes 294920 | tf_op jit(solution)/shard_map/ppermute | solution.py:17
  107.1 3.5 %collective-permute-done.6 = f32[12,2,1,1024]{3,2,1,0:T(1,128)S(1)} collective-permute-done((f32[12,2,1,1024]{3,2,1,0:T(1,128)S(1)}, f32[12,2,1,1024]{3,2,1,0:T(1,128)S(1)}, u32[]{:S(2)}, u32[]{:S(2)}) %collective-permute-start.6) | collective-permute-done | bytes 98336 | tf_op jit(solution)/shard_map/ppermute | solution.py:17
  110.9 0.5 multiply_add_fusion.3
  111.9 1.9 collective-permute-start.9
  113.8 2.6 collective-permute-start.8
  116.4 4.2 %collective-permute-done.8 = f32[12,2,1,1024]{3,2,1,0:T(1,128)S(1)} collective-permute-done((f32[12,2,1,1024]{3,2,1,0:T(1,128)S(1)}, f32[12,2,1,1024]{3,2,1,0:T(1,128)S(1)}, u32[]{:S(2)}, u32[]{:S(2)}) %collective-permute-start.8) | collective-permute-done | bytes 98336 | tf_op jit(solution)/shard_map/ppermute | solution.py:17
  120.9 0.8 fusion.31
  121.7 5.9 %copy.25 = f32[12,2,8,1024]{0,1,3,2:T(2,128)} copy(f32[12,2,8,1024]{3,2,1,0:T(8,128)S(1)} %fusion.31) | data formatting | bytes 1572864 | tf_op jit(solution)/shard_map/add | solution.py:63
  127.6 6.5 %gather_fusion.3 = f32[400,12,2]{1,2,0:T(2,128)S(1)} fusion(f32[12,2,8,1024]{0,1,3,2:T(2,128)} %copy.25, s32[400]{0:T(512)S(1)} %bitcast.31), kind=kCustom, calls=%fused_computation.3 | custom fusion | bytes 80000 | tf_op jit(solution)/shard_map/gather | solution.py:123
  134.1 0.6 fusion.41
  134.9 49.3 %psum.7 = f32[12,400]{1,0:T(8,128)S(1)} all-reduce(f32[12,400]{1,0:T(8,128)S(1)} %copy.27), channel_id=1, replica_groups=mesh['groups'=2,'tile'=16] {'tile'}, use_global_device_ids=true, to_apply=%region_6.7 | all-reduce | flops 4800 | bytes 38400 | tf_op jit(solution)/shard_map/psum | solution.py:125
  184.2 0.6 multiply_reduce_fusion.1
  186.1 5.9 %broadcast.196 = f32[12,2,8,1024]{0,1,3,2:T(2,128)} broadcast(f32[]{:T(128)} %constant.19.clone.1), dimensions={} | broadcast | bytes 786436 | tf_op jit(solution)/shard_map/broadcast.24
  192.1 39.4 %scatter_fusion.1 = f32[12,2,8,1024]{0,1,3,2:T(2,128)} fusion(f32[12,2,8,1024]{0,1,3,2:T(2,128)} %broadcast.196, s32[400]{0:T(512)S(1)} %bitcast.32, f32[400,12,2]{1,2,0:T(2,128)S(1)} %multiply_bitcast_fusion), kind=kCustom, calls=%fused_computation.5 | custom fusion | flops 9600 | bytes 118400 | tf_op jit(solution)/shard_map/scatter-add | solution.py:130
  231.5 6.9 %copy.29 = f32[12,2,8,1024]{3,2,1,0:T(8,128)S(1)} copy(f32[12,2,8,1024]{0,1,3,2:T(2,128)} %scatter_fusion.1) | data formatting | bytes 1572864 | tf_op jit(solution)/shard_map/scatter-add | solution.py:130
  238.9 4.5 %collective-permute-start.11 = (f32[12,2,1,1024]{3,2,1,0:T(1,128)S(1)}, f32[12,2,1,1024]{3,2,1,0:T(1,128)S(1)}, u32[]{:S(2)}, u32[]{:S(2)}) collective-permute-start(f32[12,2,1,1024]{3,2,1,0:T(1,128)S(1)} %get-tuple-element.30), channel_id=1, source_target_pairs={{0,1},{1,2},{2,3},{3,4},{4,5},{5,6},{6,7},{7,8},{8,9},{9,10},{10,1... | collective-permute-start | bytes 294920 | tf_op jit(solution)/shard_map/ppermute | solution.py:14
  243.4 4.3 %collective-permute-start.10 = (f32[12,2,1,1024]{3,2,1,0:T(1,128)S(1)}, f32[12,2,1,1024]{3,2,1,0:T(1,128)S(1)}, u32[]{:S(2)}, u32[]{:S(2)}) collective-permute-start(f32[12,2,1,1024]{3,2,1,0:T(1,128)S(1)} %get-tuple-element.31), channel_id=1, source_target_pairs={{1,0},{2,1},{3,2},{4,3},{5,4},{6,5},{7,6},{8,7},{9,8},{10,9},{11,1... | collective-permute-start | bytes 294920 | tf_op jit(solution)/shard_map/ppermute | solution.py:17
  247.8 2.4 collective-permute-done.10
  251.5 1.9 collective-permute-start.13
  253.4 3.6 %collective-permute-start.12 = (f32[12,2,1,1024]{3,2,1,0:T(1,128)S(1)}, f32[12,2,1,1024]{3,2,1,0:T(1,128)S(1)}, u32[]{:S(2)}, u32[]{:S(2)}) collective-permute-start(f32[12,2,1,1024]{3,2,1,0:T(1,128)S(1)} %get-tuple-element.29), channel_id=1, source_target_pairs={{1,0},{2,1},{3,2},{4,3},{5,4},{6,5},{7,6},{8,7},{9,8},{10,9},{11,1... | collective-permute-start | bytes 294920 | tf_op jit(solution)/shard_map/ppermute | solution.py:17
  257.1 3.2 %collective-permute-done.12 = f32[12,2,1,1024]{3,2,1,0:T(1,128)S(1)} collective-permute-done((f32[12,2,1,1024]{3,2,1,0:T(1,128)S(1)}, f32[12,2,1,1024]{3,2,1,0:T(1,128)S(1)}, u32[]{:S(2)}, u32[]{:S(2)}) %collective-permute-start.12) | collective-permute-done | bytes 98336 | tf_op jit(solution)/shard_map/ppermute | solution.py:17
  260.6 0.6 multiply_add_fusion.1
  261.6 1.9 collective-permute-start.15
  263.5 2.5 collective-permute-start.14
  266.1 4.3 %collective-permute-done.14 = f32[12,2,1,1024]{3,2,1,0:T(1,128)S(1)} collective-permute-done((f32[12,2,1,1024]{3,2,1,0:T(1,128)S(1)}, f32[12,2,1,1024]{3,2,1,0:T(1,128)S(1)}, u32[]{:S(2)}, u32[]{:S(2)}) %collective-permute-start.14) | collective-permute-done | bytes 98336 | tf_op jit(solution)/shard_map/ppermute | solution.py:17
  270.7 0.5 multiply_add_fusion
  271.6 1.9 collective-permute-start.17
  273.6 2.4 collective-permute-start.16
  276.1 4.4 %collective-permute-done.16 = f32[12,2,1,1024]{3,2,1,0:T(1,128)S(1)} collective-permute-done((f32[12,2,1,1024]{3,2,1,0:T(1,128)S(1)}, f32[12,2,1,1024]{3,2,1,0:T(1,128)S(1)}, u32[]{:S(2)}, u32[]{:S(2)}) %collective-permute-start.16) | collective-permute-done | bytes 98336 | tf_op jit(solution)/shard_map/ppermute | solution.py:17
  280.7 0.8 fusion.16
  281.7 1.9 collective-permute-start.18
  283.7 2.4 collective-permute-start.19
  286.1 0.5 multiply_reduce_fusion
  286.8 4.8 %collective-permute-done.19 = f32[2,12,2,1,1024]{4,3,2,1,0:T(1,128)S(1)} collective-permute-done((f32[2,12,2,1,1024]{4,3,2,1,0:T(1,128)S(1)}, f32[2,12,2,1,1024]{4,3,2,1,0:T(1,128)S(1)}, u32[]{:S(2)}, u32[]{:S(2)}) %collective-permute-start.19) | collective-permute-done | bytes 196640 | tf_op jit(solution)/shard_map/ppermute | solution.py:17
  291.6 0.6 pad_maximum_fusion
  292.5 0.6 fusion.1
  293.3 0.7 fusion.57
  (82 shorter events, 9.1 us)
Async XLA Ops:
  0.6 13.9 %copy-start.5 = (f32[12]{0:T(128)S(1)}, f32[12]{0:T(128)}, u32[]{:S(2)}) copy-start(f32[12]{0:T(128)} %param.14) | copy-start | bytes 148
  0.6 15.1 %copy-start.3 = (f32[2,8,1024]{2,1,0:T(8,128)S(1)}, f32[2,8,1024]{2,1,0:T(8,128)}, u32[]{:S(2)}) copy-start(f32[2,8,1024]{2,1,0:T(8,128)} %param.12) | copy-start | bytes 196612
  2.5 16.2 %collective-permute-start = (f32[2,2,1,1024]{3,2,1,0:T(1,128)S(1)}, f32[2,2,1,1024]{3,2,1,0:T(1,128)S(1)}, u32[]{:S(2)}, u32[]{:S(2)}) collective-permute-start(f32[2,2,1,1024]{3,2,1,0:T(1,128)S(1)} %get-tuple-element.40), channel_id=1, source_target_pairs={{0,1},{1,2},{2,3},{3,4},{4,5},{5,6},{6,7},{7,8},{8,9},{9,10},{10,1... | collective-permute-start | bytes 49160 | tf_op jit(solution)/shard_map/ppermute | solution.py:14
  6.2 12.5 %collective-permute-start.1 = (f32[2,2,1,1024]{3,2,1,0:T(1,128)S(1)}, f32[2,2,1,1024]{3,2,1,0:T(1,128)S(1)}, u32[]{:S(2)}, u32[]{:S(2)}) collective-permute-start(f32[2,2,1,1024]{3,2,1,0:T(1,128)S(1)} %get-tuple-element.41), channel_id=1, source_target_pairs={{1,0},{2,1},{3,2},{4,3},{5,4},{6,5},{7,6},{8,7},{9,8},{10,9},{11,1... | collective-permute-start | bytes 49160 | tf_op jit(solution)/shard_map/ppermute | solution.py:17
  15.8 2.9 copy-start
  80.6 6.3 %collective-permute-start.3 = (f32[12,2,1,1024]{3,2,1,0:T(1,128)}, f32[12,2,1,1024]{3,2,1,0:T(1,128)}, u32[]{:S(2)}, u32[]{:S(2)}) collective-permute-start(f32[12,2,1,1024]{3,2,1,0:T(1,128)} %get-tuple-element.38), channel_id=1, source_target_pairs={{0,1},{1,2},{2,3},{3,4},{4,5},{5,6},{6,7},{7,8},{8,9},{9,10},{10,1... | collective-permute-start | bytes 294920 | tf_op jit(solution)/shard_map/ppermute | solution.py:14
  82.5 7.0 %collective-permute-start.2 = (f32[12,2,1,1024]{3,2,1,0:T(1,128)S(1)}, f32[12,2,1,1024]{3,2,1,0:T(1,128)}, u32[]{:S(2)}, u32[]{:S(2)}) collective-permute-start(f32[12,2,1,1024]{3,2,1,0:T(1,128)S(1)} %get-tuple-element.39), channel_id=1, source_target_pairs={{1,0},{2,1},{3,2},{4,3},{5,4},{6,5},{7,6},{8,7},{9,8},{10,9},{11,1... | collective-permute-start | bytes 294920 | tf_op jit(solution)/shard_map/ppermute | solution.py:17
  91.8 6.0 %collective-permute-start.5 = (f32[12,2,1,1024]{3,2,1,0:T(1,128)S(1)}, f32[12,2,1,1024]{3,2,1,0:T(1,128)S(1)}, u32[]{:S(2)}, u32[]{:S(2)}) collective-permute-start(f32[12,2,1,1024]{3,2,1,0:T(1,128)S(1)} %get-tuple-element.36), channel_id=1, source_target_pairs={{0,1},{1,2},{2,3},{3,4},{4,5},{5,6},{6,7},{7,8},{8,9},{9,10},{10,1... | collective-permute-start | bytes 294920 | tf_op jit(solution)/shard_map/ppermute | solution.py:14
  93.7 6.8 %collective-permute-start.4 = (f32[12,2,1,1024]{3,2,1,0:T(1,128)S(1)}, f32[12,2,1,1024]{3,2,1,0:T(1,128)S(1)}, u32[]{:S(2)}, u32[]{:S(2)}) collective-permute-start(f32[12,2,1,1024]{3,2,1,0:T(1,128)S(1)} %get-tuple-element.37), channel_id=1, source_target_pairs={{1,0},{2,1},{3,2},{4,3},{5,4},{6,5},{7,6},{8,7},{9,8},{10,9},{11,1... | collective-permute-start | bytes 294920 | tf_op jit(solution)/shard_map/ppermute | solution.py:17
  101.8 5.2 %collective-permute-start.7 = (f32[12,2,1,1024]{3,2,1,0:T(1,128)S(1)}, f32[12,2,1,1024]{3,2,1,0:T(1,128)S(1)}, u32[]{:S(2)}, u32[]{:S(2)}) collective-permute-start(f32[12,2,1,1024]{3,2,1,0:T(1,128)S(1)} %get-tuple-element.34), channel_id=1, source_target_pairs={{0,1},{1,2},{2,3},{3,4},{4,5},{5,6},{6,7},{7,8},{8,9},{9,10},{10,1... | collective-permute-start | bytes 294920 | tf_op jit(solution)/shard_map/ppermute | solution.py:14
  103.7 6.8 %collective-permute-start.6 = (f32[12,2,1,1024]{3,2,1,0:T(1,128)S(1)}, f32[12,2,1,1024]{3,2,1,0:T(1,128)S(1)}, u32[]{:S(2)}, u32[]{:S(2)}) collective-permute-start(f32[12,2,1,1024]{3,2,1,0:T(1,128)S(1)} %get-tuple-element.35), channel_id=1, source_target_pairs={{1,0},{2,1},{3,2},{4,3},{5,4},{6,5},{7,6},{8,7},{9,8},{10,9},{11,1... | collective-permute-start | bytes 294920 | tf_op jit(solution)/shard_map/ppermute | solution.py:17
  111.9 4.6 %collective-permute-start.9 = (f32[12,2,1,1024]{3,2,1,0:T(1,128)S(1)}, f32[12,2,1,1024]{3,2,1,0:T(1,128)S(1)}, u32[]{:S(2)}, u32[]{:S(2)}) collective-permute-start(f32[12,2,1,1024]{3,2,1,0:T(1,128)S(1)} %get-tuple-element.32), channel_id=1, source_target_pairs={{0,1},{1,2},{2,3},{3,4},{4,5},{5,6},{6,7},{7,8},{8,9},{9,10},{10,1... | collective-permute-start | bytes 294920 | tf_op jit(solution)/shard_map/ppermute | solution.py:14
  113.8 6.8 %collective-permute-start.8 = (f32[12,2,1,1024]{3,2,1,0:T(1,128)S(1)}, f32[12,2,1,1024]{3,2,1,0:T(1,128)S(1)}, u32[]{:S(2)}, u32[]{:S(2)}) collective-permute-start(f32[12,2,1,1024]{3,2,1,0:T(1,128)S(1)} %get-tuple-element.33), channel_id=1, source_target_pairs={{1,0},{2,1},{3,2},{4,3},{5,4},{6,5},{7,6},{8,7},{9,8},{10,9},{11,1... | collective-permute-start | bytes 294920 | tf_op jit(solution)/shard_map/ppermute | solution.py:17
  121.7 62.5 %copy-start.4 = (f32[12,400]{1,0:T(8,128)S(1)}, f32[12,400]{1,0:T(8,128)}, u32[]{:S(2)}) copy-start(f32[12,400]{1,0:T(8,128)} %param.13) | copy-start | bytes 57604
  184.2 7.9 %copy-start.2 = (f32[12,400]{1,0:T(8,128)}, f32[12,400]{1,0:T(8,128)S(1)}, u32[]{:S(2)}) copy-start(f32[12,400]{1,0:T(8,128)S(1)} %psum.7) | copy-start | bytes 57604
  238.9 8.9 %collective-permute-start.11 = (f32[12,2,1,1024]{3,2,1,0:T(1,128)S(1)}, f32[12,2,1,1024]{3,2,1,0:T(1,128)S(1)}, u32[]{:S(2)}, u32[]{:S(2)}) collective-permute-start(f32[12,2,1,1024]{3,2,1,0:T(1,128)S(1)} %get-tuple-element.30), channel_id=1, source_target_pairs={{0,1},{1,2},{2,3},{3,4},{4,5},{5,6},{6,7},{7,8},{8,9},{9,10},{10,1... | collective-permute-start | bytes 294920 | tf_op jit(solution)/shard_map/ppermute | solution.py:14
  243.4 6.8 %collective-permute-start.10 = (f32[12,2,1,1024]{3,2,1,0:T(1,128)S(1)}, f32[12,2,1,1024]{3,2,1,0:T(1,128)S(1)}, u32[]{:S(2)}, u32[]{:S(2)}) collective-permute-start(f32[12,2,1,1024]{3,2,1,0:T(1,128)S(1)} %get-tuple-element.31), channel_id=1, source_target_pairs={{1,0},{2,1},{3,2},{4,3},{5,4},{6,5},{7,6},{8,7},{9,8},{10,9},{11,1... | collective-permute-start | bytes 294920 | tf_op jit(solution)/shard_map/ppermute | solution.py:17
  251.5 5.6 %collective-permute-start.13 = (f32[12,2,1,1024]{3,2,1,0:T(1,128)S(1)}, f32[12,2,1,1024]{3,2,1,0:T(1,128)S(1)}, u32[]{:S(2)}, u32[]{:S(2)}) collective-permute-start(f32[12,2,1,1024]{3,2,1,0:T(1,128)S(1)} %get-tuple-element.28), channel_id=1, source_target_pairs={{0,1},{1,2},{2,3},{3,4},{4,5},{5,6},{6,7},{7,8},{8,9},{9,10},{10,1... | collective-permute-start | bytes 294920 | tf_op jit(solution)/shard_map/ppermute | solution.py:14
  253.4 6.8 %collective-permute-start.12 = (f32[12,2,1,1024]{3,2,1,0:T(1,128)S(1)}, f32[12,2,1,1024]{3,2,1,0:T(1,128)S(1)}, u32[]{:S(2)}, u32[]{:S(2)}) collective-permute-start(f32[12,2,1,1024]{3,2,1,0:T(1,128)S(1)} %get-tuple-element.29), channel_id=1, source_target_pairs={{1,0},{2,1},{3,2},{4,3},{5,4},{6,5},{7,6},{8,7},{9,8},{10,9},{11,1... | collective-permute-start | bytes 294920 | tf_op jit(solution)/shard_map/ppermute | solution.py:17
  261.6 4.4 %collective-permute-start.15 = (f32[12,2,1,1024]{3,2,1,0:T(1,128)S(1)}, f32[12,2,1,1024]{3,2,1,0:T(1,128)S(1)}, u32[]{:S(2)}, u32[]{:S(2)}) collective-permute-start(f32[12,2,1,1024]{3,2,1,0:T(1,128)S(1)} %get-tuple-element.26), channel_id=1, source_target_pairs={{0,1},{1,2},{2,3},{3,4},{4,5},{5,6},{6,7},{7,8},{8,9},{9,10},{10,1... | collective-permute-start | bytes 294920 | tf_op jit(solution)/shard_map/ppermute | solution.py:14
  263.5 6.8 %collective-permute-start.14 = (f32[12,2,1,1024]{3,2,1,0:T(1,128)S(1)}, f32[12,2,1,1024]{3,2,1,0:T(1,128)S(1)}, u32[]{:S(2)}, u32[]{:S(2)}) collective-permute-start(f32[12,2,1,1024]{3,2,1,0:T(1,128)S(1)} %get-tuple-element.27), channel_id=1, source_target_pairs={{1,0},{2,1},{3,2},{4,3},{5,4},{6,5},{7,6},{8,7},{9,8},{10,9},{11,1... | collective-permute-start | bytes 294920 | tf_op jit(solution)/shard_map/ppermute | solution.py:17
  271.6 4.4 %collective-permute-start.17 = (f32[12,2,1,1024]{3,2,1,0:T(1,128)S(1)}, f32[12,2,1,1024]{3,2,1,0:T(1,128)S(1)}, u32[]{:S(2)}, u32[]{:S(2)}) collective-permute-start(f32[12,2,1,1024]{3,2,1,0:T(1,128)S(1)} %get-tuple-element.24), channel_id=1, source_target_pairs={{0,1},{1,2},{2,3},{3,4},{4,5},{5,6},{6,7},{7,8},{8,9},{9,10},{10,1... | collective-permute-start | bytes 294920 | tf_op jit(solution)/shard_map/ppermute | solution.py:14
  273.6 6.8 %collective-permute-start.16 = (f32[12,2,1,1024]{3,2,1,0:T(1,128)S(1)}, f32[12,2,1,1024]{3,2,1,0:T(1,128)S(1)}, u32[]{:S(2)}, u32[]{:S(2)}) collective-permute-start(f32[12,2,1,1024]{3,2,1,0:T(1,128)S(1)} %get-tuple-element.25), channel_id=1, source_target_pairs={{1,0},{2,1},{3,2},{4,3},{5,4},{6,5},{7,6},{8,7},{9,8},{10,9},{11,1... | collective-permute-start | bytes 294920 | tf_op jit(solution)/shard_map/ppermute | solution.py:17
  281.7 5.0 %collective-permute-start.18 = (f32[2,12,2,1,1024]{4,3,2,1,0:T(1,128)S(1)}, f32[2,12,2,1,1024]{4,3,2,1,0:T(1,128)S(1)}, u32[]{:S(2)}, u32[]{:S(2)}) collective-permute-start(f32[2,12,2,1,1024]{4,3,2,1,0:T(1,128)S(1)} %get-tuple-element.22), channel_id=1, source_target_pairs={{0,1},{1,2},{2,3},{3,4},{4,5},{5,6},{6,7},{7,8},{8,9},{9,10},{10,1... | collective-permute-start | bytes 589832 | tf_op jit(solution)/shard_map/ppermute | solution.py:14
  283.7 7.9 %collective-permute-start.19 = (f32[2,12,2,1,1024]{4,3,2,1,0:T(1,128)S(1)}, f32[2,12,2,1,1024]{4,3,2,1,0:T(1,128)S(1)}, u32[]{:S(2)}, u32[]{:S(2)}) collective-permute-start(f32[2,12,2,1,1024]{4,3,2,1,0:T(1,128)S(1)} %get-tuple-element.23), channel_id=1, source_target_pairs={{1,0},{2,1},{3,2},{4,3},{5,4},{6,5},{7,6},{8,7},{9,8},{10,9},{11,1... | collective-permute-start | bytes 589832 | tf_op jit(solution)/shard_map/ppermute | solution.py:17
  292.5 0.8 copy-start.1
where the time goes:
time: 296 us; the launch traced here: 294 us
  blocking collectives  108 us (36%)
  other arithmetic  63.4 us (21%)
  starting transfers between devices  53.1 us (18%)
  local copies, waits for them, and re-layouts  32.3 us (11%)
  waiting for transfers between devices  32.2 us (11%)
  between operations  5.11 us (2%)
    psum x1, blocking collectives, local(): predicted = lax.psum(local_heads, 'tile')  49.3 us
    scatter-add x1, other arithmetic, local(): adjoint_source.at[:, :, well_row, well_col]  39.4 us
    pmin x1, blocking collectives, local(): low = lax.pmin(local_low, 'tile')  32.8 us
    ppermute x10, waiting for transfers between devices, extended_2(): lax.ppermute(lax.slice_in_dim(block, 0, width, axis=dim), axis, backward)  32.2 us
    ppermute x10, starting transfers between devices, extended_2(): lax.ppermute(lax.slice_in_dim(block, 0, width, axis=dim), axis, backward)  29.6 us
    pmax x1, blocking collectives, local(): high = lax.pmax(local_high, 'tile')  25.8 us
    ppermute x10, starting transfers between devices, extended_2(): lax.ppermute(lax.slice_in_dim(block, block.shape[dim] - width, None, axis...  23.6 us
    scatter-add x1, local copies, waits for them, and re-layouts, local(): adjoint_source.at[:, :, well_row, well_col]  6.87 us
  transfers between devices with their start and end apart: 20, of which 9 were waited for; matrix products, arithmetic and copies ran while one was open for 4% of the time, Pallas kernels for 0%

commit v1 on v0

--- a/solution.py
+++ b/solution.py
@@ -122,7 +122,7 @@
     heads = solve(recharge[None] + pumping)
     sampled = heads[:, :, well_row, well_col]
     local_heads = jnp.sum(sampled * owned_weight.T[None], axis=1)
-    predicted = lax.psum(local_heads, "tile")
+    predicted = jnp.sum(lax.all_gather(local_heads, "tile"), axis=0)
     misfit = predicted - observed
     scale = jnp.sqrt(jnp.mean(misfit * misfit) + 1e-06)
     weight = misfit / scale

time: 296 us -> 262 us (0.89)
  blocking collectives: 108 us -> 76.3 us
  starting transfers between devices: 53.1 us -> 47.7 us
  waiting for transfers between devices: 32.2 us -> 35.6 us
    psum x1 -> x0, blocking collectives: 49.3 us -> none  [local(): predicted = lax.psum(local_heads, 'tile')]
    all_gather x0 -> x1, blocking collectives: none -> 17.7 us  [local(): predicted = jnp.sum(lax.all_gather(local_heads, 'tile'), axis=0)]
    ppermute x10, starting transfers between devices: 29.6 us -> 26.1 us  [extended_2(): lax.ppermute(lax.slice_in_dim(block, 0, width, axis=dim), axis, backward)]
    ppermute x10, waiting for transfers between devices: 32.2 us -> 35.6 us  [extended_2(): lax.ppermute(lax.slice_in_dim(block, 0, width, axis=dim), axis, backward)]
where the time goes in v1:
time: 262 us; the launch traced here: 260 us
  blocking collectives  76.3 us (29%)
  other arithmetic  63.4 us (24%)
  starting transfers between devices  47.7 us (18%)
  waiting for transfers between devices  35.6 us (14%)
  local copies, waits for them, and re-layouts  32.3 us (12%)
  between operations  5.12 us (2%)
    scatter-add x1, other arithmetic, local(): adjoint_source.at[:, :, well_row, well_col]  39.4 us
    ppermute x10, waiting for transfers between devices, extended_2(): lax.ppermute(lax.slice_in_dim(block, 0, width, axis=dim), axis, backward)  35.6 us
    pmin x1, blocking collectives, local(): low = lax.pmin(local_low, 'tile')  32.8 us
    ppermute x10, starting transfers between devices, extended_2(): lax.ppermute(lax.slice_in_dim(block, 0, width, axis=dim), axis, backward)  26.1 us
    pmax x1, blocking collectives, local(): high = lax.pmax(local_high, 'tile')  25.8 us
    ppermute x10, starting transfers between devices, extended_2(): lax.ppermute(lax.slice_in_dim(block, block.shape[dim] - width, None, axis...  21.5 us
    all_gather x1, blocking collectives, local(): predicted = jnp.sum(lax.all_gather(local_heads, 'tile'), axis=0)  17.7 us
    scatter-add x1, local copies, waits for them, and re-layouts, local(): adjoint_source.at[:, :, well_row, well_col]  6.87 us
  transfers between devices with their start and end apart: 20, of which 9 were waited for; matrix products, arithmetic and copies ran while one was open for 4% of the time, Pallas kernels for 0%

profile of v1, /device:TPU:5, one launch (start us, length us, event | category | flops | bytes accessed | tf_op | source)
XLA Modules:
  0.0 260.5 jit_solution(7928543162460211259)
XLA Ops:
  0.6 0.9 exponential_bitcast_fusion
  1.5 0.9 pad_maximum_fusion.7
  2.5 3.7 %collective-permute-start = (f32[2,2,1,1024]{3,2,1,0:T(1,128)S(1)}, f32[2,2,1,1024]{3,2,1,0:T(1,128)S(1)}, u32[]{:S(2)}, u32[]{:S(2)}) collective-permute-start(f32[2,2,1,1024]{3,2,1,0:T(1,128)S(1)} %get-tuple-element.38), channel_id=1, source_target_pairs={{0,1},{1,2},{2,3},{3,4},{4,5},{5,6},{6,7},{7,8},{8,9},{9,10},{10,1... | collective-permute-start | bytes 49160 | tf_op jit(solution)/shard_map/ppermute | solution.py:14
  6.2 1.9 collective-permute-start.1
  8.1 0.7 compare_select_fusion.4
  8.8 0.7 compare_select_fusion.1
  9.5 0.7 compare_select_fusion
  10.2 1.3 gather_fusion.1
  11.5 1.3 gather_fusion
  12.9 0.8 fusion.93
  13.7 0.7 compare_convert_fusion
  14.7 0.6 gather_fusion.2
  15.8 2.9 %scatter_fusion = f32[12,2,8,1024]{3,2,1,0:T(8,128)S(1)} fusion(f32[12,2,8,1024]{3,2,1,0:T(8,128)S(1)} %add.279, s32[24]{0:T(128)S(1)} %reshape.153, f32[24]{0:T(128)S(1)} %reshape.155), kind=kCustom, calls=%fused_computation.4 | custom fusion | flops 24 | bytes 672 | tf_op jit(solution)/shard_map/scatter-add | solution.py:121
  18.8 0.7 fusion.78
  19.5 25.8 %pmax.7 = f32[]{:T(128)} all-reduce(f32[]{:T(128)} %get-tuple-element.3), channel_id=1, replica_groups=mesh['groups'=2,'tile'=16] {'tile'}, use_global_device_ids=true, to_apply=%region_2.3 | all-reduce | flops 1 | bytes 8 | tf_op jit(solution)/shard_map/pmax | solution.py:93
  45.4 32.8 %pmin.7 = f32[]{:T(128)} all-reduce(f32[]{:T(128)} %get-tuple-element.2), channel_id=1, replica_groups=mesh['groups'=2,'tile'=16] {'tile'}, use_global_device_ids=true, to_apply=%region_4.5 | all-reduce | flops 1 | bytes 8 | tf_op jit(solution)/shard_map/pmin | solution.py:94
  79.5 0.8 fusion.92
  80.6 1.9 collective-permute-start.3
  82.5 2.6 collective-permute-start.2
  86.9 2.7 %collective-permute-done.2 = f32[12,2,1,1024]{3,2,1,0:T(1,128)} collective-permute-done((f32[12,2,1,1024]{3,2,1,0:T(1,128)S(1)}, f32[12,2,1,1024]{3,2,1,0:T(1,128)}, u32[]{:S(2)}, u32[]{:S(2)}) %collective-permute-start.2) | collective-permute-done | bytes 98336 | tf_op jit(solution)/shard_map/ppermute | solution.py:17
  89.6 1.2 fusion.3
  90.8 0.5 multiply_add_fusion.5
  91.8 1.9 collective-permute-start.5
  93.7 4.0 %collective-permute-start.4 = (f32[12,2,1,1024]{3,2,1,0:T(1,128)S(1)}, f32[12,2,1,1024]{3,2,1,0:T(1,128)S(1)}, u32[]{:S(2)}, u32[]{:S(2)}) collective-permute-start(f32[12,2,1,1024]{3,2,1,0:T(1,128)S(1)} %get-tuple-element.35), channel_id=1, source_target_pairs={{1,0},{2,1},{3,2},{4,3},{5,4},{6,5},{7,6},{8,7},{9,8},{10,9},{11,1... | collective-permute-start | bytes 294920 | tf_op jit(solution)/shard_map/ppermute | solution.py:17
  97.8 2.7 %collective-permute-done.4 = f32[12,2,1,1024]{3,2,1,0:T(1,128)S(1)} collective-permute-done((f32[12,2,1,1024]{3,2,1,0:T(1,128)S(1)}, f32[12,2,1,1024]{3,2,1,0:T(1,128)S(1)}, u32[]{:S(2)}, u32[]{:S(2)}) %collective-permute-start.4) | collective-permute-done | bytes 98336 | tf_op jit(solution)/shard_map/ppermute | solution.py:17
  100.8 0.5 multiply_add_fusion.4
  101.8 1.9 collective-permute-start.7
  103.7 3.3 %collective-permute-start.6 = (f32[12,2,1,1024]{3,2,1,0:T(1,128)S(1)}, f32[12,2,1,1024]{3,2,1,0:T(1,128)S(1)}, u32[]{:S(2)}, u32[]{:S(2)}) collective-permute-start(f32[12,2,1,1024]{3,2,1,0:T(1,128)S(1)} %get-tuple-element.33), channel_id=1, source_target_pairs={{1,0},{2,1},{3,2},{4,3},{5,4},{6,5},{7,6},{8,7},{9,8},{10,9},{11,1... | collective-permute-start | bytes 294920 | tf_op jit(solution)/shard_map/ppermute | solution.py:17
  107.1 3.5 %collective-permute-done.6 = f32[12,2,1,1024]{3,2,1,0:T(1,128)S(1)} collective-permute-done((f32[12,2,1,1024]{3,2,1,0:T(1,128)S(1)}, f32[12,2,1,1024]{3,2,1,0:T(1,128)S(1)}, u32[]{:S(2)}, u32[]{:S(2)}) %collective-permute-start.6) | collective-permute-done | bytes 98336 | tf_op jit(solution)/shard_map/ppermute | solution.py:17
  110.9 0.5 multiply_add_fusion.3
  111.9 1.9 collective-permute-start.9
  113.8 2.6 collective-permute-start.8
  116.4 4.2 %collective-permute-done.8 = f32[12,2,1,1024]{3,2,1,0:T(1,128)S(1)} collective-permute-done((f32[12,2,1,1024]{3,2,1,0:T(1,128)S(1)}, f32[12,2,1,1024]{3,2,1,0:T(1,128)S(1)}, u32[]{:S(2)}, u32[]{:S(2)}) %collective-permute-start.8) | collective-permute-done | bytes 98336 | tf_op jit(solution)/shard_map/ppermute | solution.py:17
  120.9 0.8 fusion.31
  121.7 5.9 %copy.25 = f32[12,2,8,1024]{0,1,3,2:T(2,128)} copy(f32[12,2,8,1024]{3,2,1,0:T(8,128)S(1)} %fusion.31) | data formatting | bytes 1572864 | tf_op jit(solution)/shard_map/add | solution.py:63
  127.6 6.5 %gather_fusion.3 = f32[400,12,2]{1,2,0:T(2,128)S(1)} fusion(f32[12,2,8,1024]{0,1,3,2:T(2,128)} %copy.25, s32[400]{0:T(512)S(1)} %bitcast.32), kind=kCustom, calls=%fused_computation.3 | custom fusion | bytes 80000 | tf_op jit(solution)/shard_map/gather | solution.py:123
  134.1 0.6 fusion.41
  134.9 17.7 %all-gather.1 = f32[16,12,400]{2,1,0:T(8,128)S(1)} all-gather(f32[1,12,400]{2,1,0:T(8,128)S(1)} %copy.27), channel_id=2, replica_groups=mesh['groups'=2,'tile'=16] {'tile'}, dimensions={0}, use_global_device_ids=true | all-gather | bytes 326400 | tf_op jit(solution)/shard_map/all_gather | solution.py:125
  152.6 0.6 multiply_reduce_fusion.1
  154.6 5.9 %broadcast.196 = f32[12,2,8,1024]{0,1,3,2:T(2,128)} broadcast(f32[]{:T(128)} %constant.19.clone.1), dimensions={} | broadcast | bytes 786436 | tf_op jit(solution)/shard_map/broadcast.24
  160.5 39.4 %scatter_fusion.1 = f32[12,2,8,1024]{0,1,3,2:T(2,128)} fusion(f32[12,2,8,1024]{0,1,3,2:T(2,128)} %broadcast.196, s32[400]{0:T(512)S(1)} %bitcast.33, f32[400,12,2]{1,2,0:T(2,128)S(1)} %multiply_bitcast_fusion), kind=kCustom, calls=%fused_computation.5 | custom fusion | flops 9600 | bytes 118400 | tf_op jit(solution)/shard_map/scatter-add | solution.py:130
  199.9 6.9 %copy.29 = f32[12,2,8,1024]{3,2,1,0:T(8,128)S(1)} copy(f32[12,2,8,1024]{0,1,3,2:T(2,128)} %scatter_fusion.1) | data formatting | bytes 1572864 | tf_op jit(solution)/shard_map/scatter-add | solution.py:130
  207.3 2.5 collective-permute-start.11
  209.8 1.9 collective-permute-start.10
  211.8 4.8 %collective-permute-done.10 = f32[12,2,1,1024]{3,2,1,0:T(1,128)S(1)} collective-permute-done((f32[12,2,1,1024]{3,2,1,0:T(1,128)S(1)}, f32[12,2,1,1024]{3,2,1,0:T(1,128)S(1)}, u32[]{:S(2)}, u32[]{:S(2)}) %collective-permute-start.10) | collective-permute-done | bytes 98336 | tf_op jit(solution)/shard_map/ppermute | solution.py:17
  217.9 1.9 collective-permute-start.13
  219.8 2.6 %collective-permute-start.12 = (f32[12,2,1,1024]{3,2,1,0:T(1,128)S(1)}, f32[12,2,1,1024]{3,2,1,0:T(1,128)S(1)}, u32[]{:S(2)}, u32[]{:S(2)}) collective-permute-start(f32[12,2,1,1024]{3,2,1,0:T(1,128)S(1)} %get-tuple-element.27), channel_id=1, source_target_pairs={{1,0},{2,1},{3,2},{4,3},{5,4},{6,5},{7,6},{8,7},{9,8},{10,9},{11,1... | collective-permute-start | bytes 294920 | tf_op jit(solution)/shard_map/ppermute | solution.py:17
  222.5 4.1 %collective-permute-done.12 = f32[12,2,1,1024]{3,2,1,0:T(1,128)S(1)} collective-permute-done((f32[12,2,1,1024]{3,2,1,0:T(1,128)S(1)}, f32[12,2,1,1024]{3,2,1,0:T(1,128)S(1)}, u32[]{:S(2)}, u32[]{:S(2)}) %collective-permute-start.12) | collective-permute-done | bytes 98336 | tf_op jit(solution)/shard_map/ppermute | solution.py:17
  227.0 0.6 multiply_add_fusion.1
  228.0 1.9 collective-permute-start.15
  229.9 2.4 collective-permute-start.14
  232.4 4.4 %collective-permute-done.14 = f32[12,2,1,1024]{3,2,1,0:T(1,128)S(1)} collective-permute-done((f32[12,2,1,1024]{3,2,1,0:T(1,128)S(1)}, f32[12,2,1,1024]{3,2,1,0:T(1,128)S(1)}, u32[]{:S(2)}, u32[]{:S(2)}) %collective-permute-start.14) | collective-permute-done | bytes 98336 | tf_op jit(solution)/shard_map/ppermute | solution.py:17
  237.1 0.5 multiply_add_fusion
  238.1 1.9 collective-permute-start.17
  240.0 2.4 collective-permute-start.16
  242.5 4.4 %collective-permute-done.16 = f32[12,2,1,1024]{3,2,1,0:T(1,128)S(1)} collective-permute-done((f32[12,2,1,1024]{3,2,1,0:T(1,128)S(1)}, f32[12,2,1,1024]{3,2,1,0:T(1,128)S(1)}, u32[]{:S(2)}, u32[]{:S(2)}) %collective-permute-start.16) | collective-permute-done | bytes 98336 | tf_op jit(solution)/shard_map/ppermute | solution.py:17
  247.1 0.8 fusion.16
  248.1 1.9 collective-permute-start.18
  250.1 2.4 collective-permute-start.19
  252.5 0.5 multiply_reduce_fusion
  253.2 4.8 %collective-permute-done.19 = f32[2,12,2,1,1024]{4,3,2,1,0:T(1,128)S(1)} collective-permute-done((f32[2,12,2,1,1024]{4,3,2,1,0:T(1,128)S(1)}, f32[2,12,2,1,1024]{4,3,2,1,0:T(1,128)S(1)}, u32[]{:S(2)}, u32[]{:S(2)}) %collective-permute-start.19) | collective-permute-done | bytes 196640 | tf_op jit(solution)/shard_map/ppermute | solution.py:17
  258.0 0.6 pad_maximum_fusion
  258.9 0.6 fusion.1
  259.8 0.7 fusion.57
  (83 shorter events, 9.1 us)
Async XLA Ops:
  0.6 13.9 %copy-start.5 = (f32[12]{0:T(128)S(1)}, f32[12]{0:T(128)}, u32[]{:S(2)}) copy-start(f32[12]{0:T(128)} %param.14) | copy-start | bytes 148
  0.6 15.1 %copy-start.3 = (f32[2,8,1024]{2,1,0:T(8,128)S(1)}, f32[2,8,1024]{2,1,0:T(8,128)}, u32[]{:S(2)}) copy-start(f32[2,8,1024]{2,1,0:T(8,128)} %param.12) | copy-start | bytes 196612
  2.5 16.2 %collective-permute-start = (f32[2,2,1,1024]{3,2,1,0:T(1,128)S(1)}, f32[2,2,1,1024]{3,2,1,0:T(1,128)S(1)}, u32[]{:S(2)}, u32[]{:S(2)}) collective-permute-start(f32[2,2,1,1024]{3,2,1,0:T(1,128)S(1)} %get-tuple-element.38), channel_id=1, source_target_pairs={{0,1},{1,2},{2,3},{3,4},{4,5},{5,6},{6,7},{7,8},{8,9},{9,10},{10,1... | collective-permute-start | bytes 49160 | tf_op jit(solution)/shard_map/ppermute | solution.py:14
  6.2 12.5 %collective-permute-start.1 = (f32[2,2,1,1024]{3,2,1,0:T(1,128)S(1)}, f32[2,2,1,1024]{3,2,1,0:T(1,128)S(1)}, u32[]{:S(2)}, u32[]{:S(2)}) collective-permute-start(f32[2,2,1,1024]{3,2,1,0:T(1,128)S(1)} %get-tuple-element.39), channel_id=1, source_target_pairs={{1,0},{2,1},{3,2},{4,3},{5,4},{6,5},{7,6},{8,7},{9,8},{10,9},{11,1... | collective-permute-start | bytes 49160 | tf_op jit(solution)/shard_map/ppermute | solution.py:17
  15.8 2.9 %copy-start = (f32[2,8,1024]{2,1,0:T(8,128)S(1)}, f32[2,8,1024]{2,1,0:T(8,128)}, u32[]{:S(2)}) copy-start(f32[2,8,1024]{2,1,0:T(8,128)} %param.11) | copy-start | bytes 196612
  80.6 6.3 %collective-permute-start.3 = (f32[12,2,1,1024]{3,2,1,0:T(1,128)}, f32[12,2,1,1024]{3,2,1,0:T(1,128)}, u32[]{:S(2)}, u32[]{:S(2)}) collective-permute-start(f32[12,2,1,1024]{3,2,1,0:T(1,128)} %get-tuple-element.36), channel_id=1, source_target_pairs={{0,1},{1,2},{2,3},{3,4},{4,5},{5,6},{6,7},{7,8},{8,9},{9,10},{10,1... | collective-permute-start | bytes 294920 | tf_op jit(solution)/shard_map/ppermute | solution.py:14
  82.5 7.0 %collective-permute-start.2 = (f32[12,2,1,1024]{3,2,1,0:T(1,128)S(1)}, f32[12,2,1,1024]{3,2,1,0:T(1,128)}, u32[]{:S(2)}, u32[]{:S(2)}) collective-permute-start(f32[12,2,1,1024]{3,2,1,0:T(1,128)S(1)} %get-tuple-element.37), channel_id=1, source_target_pairs={{1,0},{2,1},{3,2},{4,3},{5,4},{6,5},{7,6},{8,7},{9,8},{10,9},{11,1... | collective-permute-start | bytes 294920 | tf_op jit(solution)/shard_map/ppermute | solution.py:17
  91.8 6.0 %collective-permute-start.5 = (f32[12,2,1,1024]{3,2,1,0:T(1,128)S(1)}, f32[12,2,1,1024]{3,2,1,0:T(1,128)S(1)}, u32[]{:S(2)}, u32[]{:S(2)}) collective-permute-start(f32[12,2,1,1024]{3,2,1,0:T(1,128)S(1)} %get-tuple-element.34), channel_id=1, source_target_pairs={{0,1},{1,2},{2,3},{3,4},{4,5},{5,6},{6,7},{7,8},{8,9},{9,10},{10,1... | collective-permute-start | bytes 294920 | tf_op jit(solution)/shard_map/ppermute | solution.py:14
  93.7 6.8 %collective-permute-start.4 = (f32[12,2,1,1024]{3,2,1,0:T(1,128)S(1)}, f32[12,2,1,1024]{3,2,1,0:T(1,128)S(1)}, u32[]{:S(2)}, u32[]{:S(2)}) collective-permute-start(f32[12,2,1,1024]{3,2,1,0:T(1,128)S(1)} %get-tuple-element.35), channel_id=1, source_target_pairs={{1,0},{2,1},{3,2},{4,3},{5,4},{6,5},{7,6},{8,7},{9,8},{10,9},{11,1... | collective-permute-start | bytes 294920 | tf_op jit(solution)/shard_map/ppermute | solution.py:17
  101.8 5.2 %collective-permute-start.7 = (f32[12,2,1,1024]{3,2,1,0:T(1,128)S(1)}, f32[12,2,1,1024]{3,2,1,0:T(1,128)S(1)}, u32[]{:S(2)}, u32[]{:S(2)}) collective-permute-start(f32[12,2,1,1024]{3,2,1,0:T(1,128)S(1)} %get-tuple-element.32), channel_id=1, source_target_pairs={{0,1},{1,2},{2,3},{3,4},{4,5},{5,6},{6,7},{7,8},{8,9},{9,10},{10,1... | collective-permute-start | bytes 294920 | tf_op jit(solution)/shard_map/ppermute | solution.py:14
  103.7 6.8 %collective-permute-start.6 = (f32[12,2,1,1024]{3,2,1,0:T(1,128)S(1)}, f32[12,2,1,1024]{3,2,1,0:T(1,128)S(1)}, u32[]{:S(2)}, u32[]{:S(2)}) collective-permute-start(f32[12,2,1,1024]{3,2,1,0:T(1,128)S(1)} %get-tuple-element.33), channel_id=1, source_target_pairs={{1,0},{2,1},{3,2},{4,3},{5,4},{6,5},{7,6},{8,7},{9,8},{10,9},{11,1... | collective-permute-start | bytes 294920 | tf_op jit(solution)/shard_map/ppermute | solution.py:17
  111.9 4.6 %collective-permute-start.9 = (f32[12,2,1,1024]{3,2,1,0:T(1,128)S(1)}, f32[12,2,1,1024]{3,2,1,0:T(1,128)S(1)}, u32[]{:S(2)}, u32[]{:S(2)}) collective-permute-start(f32[12,2,1,1024]{3,2,1,0:T(1,128)S(1)} %get-tuple-element.30), channel_id=1, source_target_pairs={{0,1},{1,2},{2,3},{3,4},{4,5},{5,6},{6,7},{7,8},{8,9},{9,10},{10,1... | collective-permute-start | bytes 294920 | tf_op jit(solution)/shard_map/ppermute | solution.py:14
  113.8 6.8 %collective-permute-start.8 = (f32[12,2,1,1024]{3,2,1,0:T(1,128)S(1)}, f32[12,2,1,1024]{3,2,1,0:T(1,128)S(1)}, u32[]{:S(2)}, u32[]{:S(2)}) collective-permute-start(f32[12,2,1,1024]{3,2,1,0:T(1,128)S(1)} %get-tuple-element.31), channel_id=1, source_target_pairs={{1,0},{2,1},{3,2},{4,3},{5,4},{6,5},{7,6},{8,7},{9,8},{10,9},{11,1... | collective-permute-start | bytes 294920 | tf_op jit(solution)/shard_map/ppermute | solution.py:17
  127.6 25.0 %copy-start.4 = (f32[12,400]{1,0:T(8,128)S(1)}, f32[12,400]{1,0:T(8,128)}, u32[]{:S(2)}) copy-start(f32[12,400]{1,0:T(8,128)} %param.13) | copy-start | bytes 57604
  152.6 7.9 %copy-start.2 = (f32[12,400]{1,0:T(8,128)}, f32[12,400]{1,0:T(8,128)S(1)}, u32[]{:S(2)}) copy-start(f32[12,400]{1,0:T(8,128)S(1)} %reduce_sum.57) | copy-start | bytes 57604
  207.3 4.5 %collective-permute-start.11 = (f32[12,2,1,1024]{3,2,1,0:T(1,128)S(1)}, f32[12,2,1,1024]{3,2,1,0:T(1,128)S(1)}, u32[]{:S(2)}, u32[]{:S(2)}) collective-permute-start(f32[12,2,1,1024]{3,2,1,0:T(1,128)S(1)} %get-tuple-element.28), channel_id=1, source_target_pairs={{0,1},{1,2},{2,3},{3,4},{4,5},{5,6},{6,7},{7,8},{8,9},{9,10},{10,1... | collective-permute-start | bytes 294920 | tf_op jit(solution)/shard_map/ppermute | solution.py:14
  209.8 6.8 %collective-permute-start.10 = (f32[12,2,1,1024]{3,2,1,0:T(1,128)S(1)}, f32[12,2,1,1024]{3,2,1,0:T(1,128)S(1)}, u32[]{:S(2)}, u32[]{:S(2)}) collective-permute-start(f32[12,2,1,1024]{3,2,1,0:T(1,128)S(1)} %get-tuple-element.29), channel_id=1, source_target_pairs={{1,0},{2,1},{3,2},{4,3},{5,4},{6,5},{7,6},{8,7},{9,8},{10,9},{11,1... | collective-permute-start | bytes 294920 | tf_op jit(solution)/shard_map/ppermute | solution.py:17
  217.9 4.6 %collective-permute-start.13 = (f32[12,2,1,1024]{3,2,1,0:T(1,128)S(1)}, f32[12,2,1,1024]{3,2,1,0:T(1,128)S(1)}, u32[]{:S(2)}, u32[]{:S(2)}) collective-permute-start(f32[12,2,1,1024]{3,2,1,0:T(1,128)S(1)} %get-tuple-element.26), channel_id=1, source_target_pairs={{0,1},{1,2},{2,3},{3,4},{4,5},{5,6},{6,7},{7,8},{8,9},{9,10},{10,1... | collective-permute-start | bytes 294920 | tf_op jit(solution)/shard_map/ppermute | solution.py:14
  219.8 6.8 %collective-permute-start.12 = (f32[12,2,1,1024]{3,2,1,0:T(1,128)S(1)}, f32[12,2,1,1024]{3,2,1,0:T(1,128)S(1)}, u32[]{:S(2)}, u32[]{:S(2)}) collective-permute-start(f32[12,2,1,1024]{3,2,1,0:T(1,128)S(1)} %get-tuple-element.27), channel_id=1, source_target_pairs={{1,0},{2,1},{3,2},{4,3},{5,4},{6,5},{7,6},{8,7},{9,8},{10,9},{11,1... | collective-permute-start | bytes 294920 | tf_op jit(solution)/shard_map/ppermute | solution.py:17
  228.0 4.4 %collective-permute-start.15 = (f32[12,2,1,1024]{3,2,1,0:T(1,128)S(1)}, f32[12,2,1,1024]{3,2,1,0:T(1,128)S(1)}, u32[]{:S(2)}, u32[]{:S(2)}) collective-permute-start(f32[12,2,1,1024]{3,2,1,0:T(1,128)S(1)} %get-tuple-element.24), channel_id=1, source_target_pairs={{0,1},{1,2},{2,3},{3,4},{4,5},{5,6},{6,7},{7,8},{8,9},{9,10},{10,1... | collective-permute-start | bytes 294920 | tf_op jit(solution)/shard_map/ppermute | solution.py:14
  229.9 6.8 %collective-permute-start.14 = (f32[12,2,1,1024]{3,2,1,0:T(1,128)S(1)}, f32[12,2,1,1024]{3,2,1,0:T(1,128)S(1)}, u32[]{:S(2)}, u32[]{:S(2)}) collective-permute-start(f32[12,2,1,1024]{3,2,1,0:T(1,128)S(1)} %get-tuple-element.25), channel_id=1, source_target_pairs={{1,0},{2,1},{3,2},{4,3},{5,4},{6,5},{7,6},{8,7},{9,8},{10,9},{11,1... | collective-permute-start | bytes 294920 | tf_op jit(solution)/shard_map/ppermute | solution.py:17
  238.1 4.4 %collective-permute-start.17 = (f32[12,2,1,1024]{3,2,1,0:T(1,128)S(1)}, f32[12,2,1,1024]{3,2,1,0:T(1,128)S(1)}, u32[]{:S(2)}, u32[]{:S(2)}) collective-permute-start(f32[12,2,1,1024]{3,2,1,0:T(1,128)S(1)} %get-tuple-element.22), channel_id=1, source_target_pairs={{0,1},{1,2},{2,3},{3,4},{4,5},{5,6},{6,7},{7,8},{8,9},{9,10},{10,1... | collective-permute-start | bytes 294920 | tf_op jit(solution)/shard_map/ppermute | solution.py:14
  240.0 6.8 %collective-permute-start.16 = (f32[12,2,1,1024]{3,2,1,0:T(1,128)S(1)}, f32[12,2,1,1024]{3,2,1,0:T(1,128)S(1)}, u32[]{:S(2)}, u32[]{:S(2)}) collective-permute-start(f32[12,2,1,1024]{3,2,1,0:T(1,128)S(1)} %get-tuple-element.23), channel_id=1, source_target_pairs={{1,0},{2,1},{3,2},{4,3},{5,4},{6,5},{7,6},{8,7},{9,8},{10,9},{11,1... | collective-permute-start | bytes 294920 | tf_op jit(solution)/shard_map/ppermute | solution.py:17
  248.1 5.0 %collective-permute-start.18 = (f32[2,12,2,1,1024]{4,3,2,1,0:T(1,128)S(1)}, f32[2,12,2,1,1024]{4,3,2,1,0:T(1,128)S(1)}, u32[]{:S(2)}, u32[]{:S(2)}) collective-permute-start(f32[2,12,2,1,1024]{4,3,2,1,0:T(1,128)S(1)} %get-tuple-element.20), channel_id=1, source_target_pairs={{0,1},{1,2},{2,3},{3,4},{4,5},{5,6},{6,7},{7,8},{8,9},{9,10},{10,1... | collective-permute-start | bytes 589832 | tf_op jit(solution)/shard_map/ppermute | solution.py:14
  250.1 7.9 %collective-permute-start.19 = (f32[2,12,2,1,1024]{4,3,2,1,0:T(1,128)S(1)}, f32[2,12,2,1,1024]{4,3,2,1,0:T(1,128)S(1)}, u32[]{:S(2)}, u32[]{:S(2)}) collective-permute-start(f32[2,12,2,1,1024]{4,3,2,1,0:T(1,128)S(1)} %get-tuple-element.21), channel_id=1, source_target_pairs={{1,0},{2,1},{3,2},{4,3},{5,4},{6,5},{7,6},{8,7},{9,8},{10,9},{11,1... | collective-permute-start | bytes 589832 | tf_op jit(solution)/shard_map/ppermute | solution.py:17
  258.9 0.8 copy-start.1
